TPU v7x, 768 devices: a whole 4x8x12 slice. The times are simulated.
768 devices in a mesh: dp: 128 (over z_hi, y, x, core), tensor: 6 (over z_lo).
Axes of the slice: x: 4, y: 8, z: 12 (z_hi: 2, z_lo: 6; z = z_hi * 6 + z_lo), core: 2. Of those that a mesh axis runs over, the one named last changes fastest.
Arguments:
- queries: bfloat16 [192, 128, 6144], P(None, 'dp', 'tensor')
- keys_values: bfloat16 [192, 128, 2048], P('tensor', 'dp')
- lengths: int32 [128], replicated, may hold values from 48 to 192
- route: int32 [1], replicated, may hold values from 1 to 7
- cotangent: bfloat16 [192, 128, 6144], P(None, 'dp', 'tensor'), may hold values from -6 to 6
- advantage: int32 [192, 128], P(None, 'dp'), may hold values from -1024 to 1024
Outputs:
- query_grads: bfloat16 [192, 128, 6144], P(None, 'dp', 'tensor')
- kv_grads: bfloat16 [192, 128, 2048], P('tensor', 'dp')
Inputs may be any that keep to these rules, and one draw needn't show every extreme that they name: route is one code for all micro-batches; a shard and its partner lie in the same aligned group of 8 shards.
All inputs are finite; a program needn't handle non-finite values.
Results may differ from a plain program's by a relative error of at most 0.038.
Values may be sent and summed in bfloat16 or wider, within the bound.
A program may use at most 32 MiB of HBM per device.

v0:
```python
import jax
import jax.numpy as jnp
from jax import lax
from jax.sharding import PartitionSpec as P

HEAD_DIM = 128


def from_partner(x, axis, apart):
    return lax.ppermute(x, axis, [(i, i ^ 1 << apart) for i in range(lax.axis_size(axis))])


def attend_one(query, keyval, grad, length):
    slot, qwidth = query.shape
    kvw = keyval.shape[1] // 2
    kvh = kvw // HEAD_DIM
    groups = qwidth // kvw
    scale = 1.0 / HEAD_DIM**0.5
    qh = query.reshape(slot, groups, kvh, HEAD_DIM)
    kh = keyval[:, :kvw].reshape(slot, kvh, HEAD_DIM)
    vh = keyval[:, kvw:].reshape(slot, kvh, HEAD_DIM)
    gh = grad.reshape(slot, groups, kvh, HEAD_DIM)
    scores = jnp.einsum("pgkd,qkd->gkpq", qh, kh, preferred_element_type=jnp.float32) * scale
    place = jnp.arange(slot)
    allowed = (place[None, :] <= place[:, None]) & (place[None, :] < length)
    scores = jnp.where(allowed[None, None], scores, -1e30)
    top = jnp.max(scores, axis=-1, keepdims=True)
    expo = jnp.exp(scores - top)
    probs = expo / jnp.sum(expo, axis=-1, keepdims=True)
    probs_b = probs.astype(jnp.bfloat16)
    attn = jnp.einsum("gkpq,qkd->pgkd", probs_b, vh, preferred_element_type=jnp.float32)
    delta = jnp.sum(gh.astype(jnp.float32) * attn, axis=-1)
    dprob = jnp.einsum("pgkd,qkd->gkpq", gh, vh, preferred_element_type=jnp.float32)
    dscore = (probs * (dprob - jnp.transpose(delta, (1, 2, 0))[..., None])).astype(jnp.bfloat16)
    dquery = jnp.einsum("gkpq,qkd->pgkd", dscore, kh, preferred_element_type=jnp.float32) * scale
    dquery = dquery.astype(jnp.bfloat16).reshape(slot, qwidth)
    dkey = jnp.einsum("gkpq,pgkd->qkd", dscore, qh, preferred_element_type=jnp.float32) * scale
    dval = jnp.einsum("gkpq,pgkd->qkd", probs_b, gh, preferred_element_type=jnp.float32)
    term = jnp.concatenate([dkey.reshape(slot, kvw), dval.reshape(slot, kvw)], axis=-1)
    return (dquery, term)


def attend(query, keyval, slot_len, grad):
    gathered = lax.all_gather(keyval, "tensor", axis=0, tiled=True)
    dquery, term = attend_one(query[:, 0], gathered[:, 0], grad[:, 0], slot_len[0])
    query_parts = [dquery]
    term_parts = [term]
    dquery = jnp.stack(query_parts, axis=1)
    terms = jnp.stack(term_parts, axis=1)
    dkv = lax.psum_scatter(terms.astype(jnp.bfloat16), "tensor", scatter_dimension=0, tiled=True)
    return (dquery, dkv)


def on_device(queries, keys_values, lengths, route, cotangent, advantage):
    slot, rolls, qwidth = queries.shape
    nbits = 3
    shard = lax.axis_index("dp")
    code = route[0]
    home_len = lax.dynamic_slice_in_dim(lengths, shard * rolls, rolls)
    partner = jnp.bitwise_xor(shard, code)
    moved_len = lax.dynamic_slice_in_dim(lengths, partner * rolls, 1)
    slot_len = jnp.concatenate([moved_len, home_len[1:]])
    count = jnp.sum(slot_len).astype(jnp.float32)
    factor = rolls * slot / count
    positions = jnp.arange(slot)
    live = (positions[:, None] < slot_len[None, :]).astype(jnp.float32)
    weight = advantage.astype(jnp.float32) / 256.0 * factor * live
    grad_out = (cotangent.astype(jnp.float32) * weight[:, :, None]).astype(jnp.bfloat16)
    front_q = queries[:, 0]
    front_kv = keys_values[:, 0]
    for bit in range(nbits):
        other_q, other_kv = from_partner((front_q, front_kv), "dp", bit)
        taken = code >> bit & 1 == 1
        front_q = jnp.where(taken, other_q, front_q)
        front_kv = jnp.where(taken, other_kv, front_kv)
    query_here = jnp.concatenate([front_q[:, None], queries[:, 1:]], axis=1)
    keyval_here = jnp.concatenate([front_kv[:, None], keys_values[:, 1:]], axis=1)
    dquery, dkv = attend(query_here, keyval_here, slot_len, grad_out)
    back_q = dquery[:, 0]
    back_kv = dkv[:, 0]
    for bit in range(nbits):
        other_q, other_kv = from_partner((back_q, back_kv), "dp", bit)
        taken = code >> bit & 1 == 1
        back_q = jnp.where(taken, other_q, back_q)
        back_kv = jnp.where(taken, other_kv, back_kv)
    query_grads = jnp.concatenate([back_q[:, None], dquery[:, 1:]], axis=1)
    kv_grads = jnp.concatenate([back_kv[:, None], dkv[:, 1:]], axis=1)
    return (query_grads, kv_grads)


def solution(mesh):
    placed = (
        P(None, "dp", "tensor"),
        P("tensor", "dp", None),
        P(),
        P(),
        P(None, "dp", "tensor"),
        P(None, "dp"),
    )
    return jax.shard_map(
        on_device,
        mesh=mesh,
        in_specs=placed,
        out_specs=(P(None, "dp", "tensor"), P("tensor", "dp", None)),
        check_vma=False,
    )
```

profile of v0, /device:TPU:4, one launch (start us, length us, event | category | flops | bytes accessed | tf_op | source)
XLA Modules:
  0.0 182.0 jit_solution(10145789430080578733)
XLA Ops:
  7.2 1.9 %collective-permute-start = (bf16[32,2048]{1,0:T(8,128)(2,1)}, bf16[32,2048]{1,0:T(8,128)(2,1)S(1)}, u32[]{:S(2)}, u32[]{:S(2)}) collective-permute-start(bf16[32,2048]{1,0:T(8,128)(2,1)} %bitcast.118), channel_id=1, source_target_pairs={{0,6},{6,0},{12,18},{18,12},{24,30},{30,24},{36,42},{42,36},{48,54... | collective-permute-start | bytes 393224 | tf_op jit(solution)/shard_map/ppermute | solution.py:10
  9.1 2.4 %collective-permute-start.3 = (bf16[192,1024]{1,0:T(8,128)(2,1)}, bf16[192,1024]{1,0:T(8,128)(2,1)S(1)}, u32[]{:S(2)}, u32[]{:S(2)}) collective-permute-start(bf16[192,1024]{1,0:T(8,128)(2,1)} %bitcast.117), channel_id=1, source_target_pairs={{0,6},{6,0},{12,18},{18,12},{24,30},{30,24},{36,42},{42,36},{48,54... | collective-permute-start | bytes 1179656 | tf_op jit(solution)/shard_map/ppermute | solution.py:10
  12.2 1.2 dynamic_slice.3
  14.1 1.3 compare_select_fusion
  15.5 1.2 fusion.29
  16.9 0.7 iota_compare_fusion.1
  17.7 3.1 %collective-permute-start.1 = (bf16[32,2048]{1,0:T(8,128)(2,1)S(1)}, bf16[32,2048]{1,0:T(8,128)(2,1)S(1)}, u32[]{:S(2)}, u32[]{:S(2)}) collective-permute-start(bf16[32,2048]{1,0:T(8,128)(2,1)S(1)} %broadcast_select_fusion.5), channel_id=1, source_target_pairs={{0,12},{6,18},{12,0},{18,6},{24,36},{30,42},{36,24},{42,30},{48,60... | collective-permute-start | bytes 393224 | tf_op jit(solution)/shard_map/ppermute | solution.py:10
  20.9 4.1 %collective-permute-done.1 = bf16[32,2048]{1,0:T(8,128)(2,1)S(1)} collective-permute-done((bf16[32,2048]{1,0:T(8,128)(2,1)S(1)}, bf16[32,2048]{1,0:T(8,128)(2,1)S(1)}, u32[]{:S(2)}, u32[]{:S(2)}) %collective-permute-start.1) | collective-permute-done | bytes 131104 | tf_op jit(solution)/shard_map/ppermute | solution.py:10
  25.0 11.4 %collective-permute-start.2 = (bf16[32,2048]{1,0:T(8,128)(2,1)S(1)}, bf16[32,2048]{1,0:T(8,128)(2,1)S(1)}, u32[]{:S(2)}, u32[]{:S(2)}) collective-permute-start(bf16[32,2048]{1,0:T(8,128)(2,1)S(1)} %broadcast_select_fusion.7), channel_id=1, source_target_pairs={{0,24},{6,30},{12,36},{18,42},{24,0},{30,6},{36,12},{42,18},{48,72... | collective-permute-start | bytes 393224 | tf_op jit(solution)/shard_map/ppermute | solution.py:10
  36.5 2.8 %collective-permute-start.4 = (bf16[192,1024]{1,0:T(8,128)(2,1)S(1)}, bf16[192,1024]{1,0:T(8,128)(2,1)S(1)}, u32[]{:S(2)}, u32[]{:S(2)}) collective-permute-start(bf16[192,1024]{1,0:T(8,128)(2,1)S(1)} %broadcast_select_fusion.1), channel_id=1, source_target_pairs={{0,12},{6,18},{12,0},{18,6},{24,36},{30,42},{36,24},{42,30},{48,60... | collective-permute-start | bytes 1179656 | tf_op jit(solution)/shard_map/ppermute | solution.py:10
  39.3 0.7 collective-permute-done.2
  40.0 8.7 %collective-permute-done.4 = bf16[192,1024]{1,0:T(8,128)(2,1)S(1)} collective-permute-done((bf16[192,1024]{1,0:T(8,128)(2,1)S(1)}, bf16[192,1024]{1,0:T(8,128)(2,1)S(1)}, u32[]{:S(2)}, u32[]{:S(2)}) %collective-permute-start.4) | collective-permute-done | bytes 393248 | tf_op jit(solution)/shard_map/ppermute | solution.py:10
  48.7 1.9 %collective-permute-start.5 = (bf16[192,1024]{1,0:T(8,128)(2,1)S(1)}, bf16[192,1024]{1,0:T(8,128)(2,1)S(1)}, u32[]{:S(2)}, u32[]{:S(2)}) collective-permute-start(bf16[192,1024]{1,0:T(8,128)(2,1)S(1)} %broadcast_select_fusion.3), channel_id=1, source_target_pairs={{0,24},{6,30},{12,36},{18,42},{24,0},{30,6},{36,12},{42,18},{48,72... | collective-permute-start | bytes 1179656 | tf_op jit(solution)/shard_map/ppermute | solution.py:10
  50.7 32.8 %all-gather = bf16[192,2048]{1,0:T(8,128)(2,1)S(1)} all-gather(bf16[32,2048]{1,0:T(8,128)(2,1)S(1)} %broadcast_select_fusion.8), channel_id=2, replica_groups=mesh['dp'=128,'tensor'=6] {'tensor'}, dimensions={0}, use_global_device_ids=true | all-gather | bytes 917504 | tf_op jit(solution)/shard_map/all_gather | solution.py:44
  83.5 0.8 slice_bitcast_fusion
  86.3 0.9 concatenate.16
  87.3 1.7 fusion.7
  89.0 0.5 fusion.3
  91.1 1.0 pad_maximum_fusion
  92.9 1.9 %collective-permute-start.6 = (bf16[192,1024]{1,0:T(8,128)(2,1)S(1)}, bf16[192,1024]{1,0:T(8,128)(2,1)S(1)}, u32[]{:S(2)}, u32[]{:S(2)}) collective-permute-start(bf16[192,1024]{1,0:T(8,128)(2,1)S(1)} %bitcast.116), channel_id=1, source_target_pairs={{0,6},{6,0},{12,18},{18,12},{24,30},{30,24},{36,42},{42,36},{48,54... | collective-permute-start | bytes 1179656 | tf_op jit(solution)/shard_map/ppermute | solution.py:10
  94.9 47.2 %reduce-scatter.2.cloned.1.call-done = bf16[32,1,2048]{2,0,1:T(8,128)(2,1)} async-done(((bf16[192,1,2048]{2,0,1:T(8,128)(2,1)}), bf16[32,1,2048]{2,0,1:T(8,128)(2,1)}) %reduce-scatter.2.cloned.1.call-update) | async-done | bytes 131088 | tf_op jit(solution)/shard_map/reduce_scatter | solution.py:50
  142.1 1.9 %collective-permute-start.9 = (bf16[32,2048]{1,0:T(8,128)(2,1)}, bf16[32,2048]{1,0:T(8,128)(2,1)S(1)}, u32[]{:S(2)}, u32[]{:S(2)}) collective-permute-start(bf16[32,2048]{1,0:T(8,128)(2,1)} %bitcast.119), channel_id=1, source_target_pairs={{0,6},{6,0},{12,18},{18,12},{24,30},{30,24},{36,42},{42,36},{48,54... | collective-permute-start | bytes 393224 | tf_op jit(solution)/shard_map/ppermute | solution.py:10
  144.1 2.9 %collective-permute-start.7 = (bf16[192,1024]{1,0:T(8,128)(2,1)S(1)}, bf16[192,1024]{1,0:T(8,128)(2,1)S(1)}, u32[]{:S(2)}, u32[]{:S(2)}) collective-permute-start(bf16[192,1024]{1,0:T(8,128)(2,1)S(1)} %broadcast_select_fusion), channel_id=1, source_target_pairs={{0,12},{6,18},{12,0},{18,6},{24,36},{30,42},{36,24},{42,30},{48,60... | collective-permute-start | bytes 1179656 | tf_op jit(solution)/shard_map/ppermute | solution.py:10
  147.0 0.9 broadcast_select_fusion.4
  147.9 2.9 %collective-permute-start.10 = (bf16[32,2048]{1,0:T(8,128)(2,1)S(1)}, bf16[32,2048]{1,0:T(8,128)(2,1)S(1)}, u32[]{:S(2)}, u32[]{:S(2)}) collective-permute-start(bf16[32,2048]{1,0:T(8,128)(2,1)S(1)} %broadcast_select_fusion.4), channel_id=1, source_target_pairs={{0,12},{6,18},{12,0},{18,6},{24,36},{30,42},{36,24},{42,30},{48,60... | collective-permute-start | bytes 393224 | tf_op jit(solution)/shard_map/ppermute | solution.py:10
  150.9 7.0 %collective-permute-done.7 = bf16[192,1024]{1,0:T(8,128)(2,1)S(1)} collective-permute-done((bf16[192,1024]{1,0:T(8,128)(2,1)S(1)}, bf16[192,1024]{1,0:T(8,128)(2,1)S(1)}, u32[]{:S(2)}, u32[]{:S(2)}) %collective-permute-start.7) | collective-permute-done | bytes 393248 | tf_op jit(solution)/shard_map/ppermute | solution.py:10
  157.9 2.5 %collective-permute-start.8 = (bf16[192,1024]{1,0:T(8,128)(2,1)S(1)}, bf16[192,1024]{1,0:T(8,128)(2,1)S(1)}, u32[]{:S(2)}, u32[]{:S(2)}) collective-permute-start(bf16[192,1024]{1,0:T(8,128)(2,1)S(1)} %broadcast_select_fusion.2), channel_id=1, source_target_pairs={{0,24},{6,30},{12,36},{18,42},{24,0},{30,6},{36,12},{42,18},{48,72... | collective-permute-start | bytes 1179656 | tf_op jit(solution)/shard_map/ppermute | solution.py:10
  160.4 4.9 %collective-permute-start.11 = (bf16[32,2048]{1,0:T(8,128)(2,1)S(1)}, bf16[32,2048]{1,0:T(8,128)(2,1)S(1)}, u32[]{:S(2)}, u32[]{:S(2)}) collective-permute-start(bf16[32,2048]{1,0:T(8,128)(2,1)S(1)} %broadcast_select_fusion.6), channel_id=1, source_target_pairs={{0,24},{6,30},{12,36},{18,42},{24,0},{30,6},{36,12},{42,18},{48,72... | collective-permute-start | bytes 393224 | tf_op jit(solution)/shard_map/ppermute | solution.py:10
  165.3 7.7 %collective-permute-done.8 = bf16[192,1024]{1,0:T(8,128)(2,1)S(1)} collective-permute-done((bf16[192,1024]{1,0:T(8,128)(2,1)S(1)}, bf16[192,1024]{1,0:T(8,128)(2,1)S(1)}, u32[]{:S(2)}, u32[]{:S(2)}) %collective-permute-start.8) | collective-permute-done | bytes 393248 | tf_op jit(solution)/shard_map/ppermute | solution.py:10
  173.1 0.8 select_bitcast_fusion
  173.8 0.6 collective-permute-done.11
  174.5 0.7 select_bitcast_fusion.2
  (54 shorter events, 5.0 us)
Async XLA Ops:
  7.2 134.9 %reduce-scatter.2.cloned.1.call-start = ((), (), s32[]{:S(2)}) async-start(), calls=%async_computation.1 | async-start | bytes 917504 | tf_op jit(solution)/shard_map/reduce_scatter | solution.py:50
  7.2 10.4 %collective-permute-start = (bf16[32,2048]{1,0:T(8,128)(2,1)}, bf16[32,2048]{1,0:T(8,128)(2,1)S(1)}, u32[]{:S(2)}, u32[]{:S(2)}) collective-permute-start(bf16[32,2048]{1,0:T(8,128)(2,1)} %bitcast.118), channel_id=1, source_target_pairs={{0,6},{6,0},{12,18},{18,12},{24,30},{30,24},{36,42},{42,36},{48,54... | collective-permute-start | bytes 393224 | tf_op jit(solution)/shard_map/ppermute | solution.py:10
  9.1 27.3 %collective-permute-start.3 = (bf16[192,1024]{1,0:T(8,128)(2,1)}, bf16[192,1024]{1,0:T(8,128)(2,1)S(1)}, u32[]{:S(2)}, u32[]{:S(2)}) collective-permute-start(bf16[192,1024]{1,0:T(8,128)(2,1)} %bitcast.117), channel_id=1, source_target_pairs={{0,6},{6,0},{12,18},{18,12},{24,30},{30,24},{36,42},{42,36},{48,54... | collective-permute-start | bytes 1179656 | tf_op jit(solution)/shard_map/ppermute | solution.py:10
  16.6 1.0 copy-start.9
  16.7 19.8 %copy-start.6 = (bf16[192,1,1024]{2,0,1:T(8,128)(2,1)S(1)}, bf16[192,1,1024]{2,0,1:T(8,128)(2,1)}, u32[]{:S(2)}) copy-start(bf16[192,1,1024]{2,0,1:T(8,128)(2,1)} %param.6) | copy-start | bytes 1179652
  16.8 68.9 %copy-start = (bf16[24,8,8,128]{3,2,1,0:T(8,128)(2,1)}, bf16[24,8,8,128]{3,2,1,0:T(8,128)(2,1)S(1)}, u32[]{:S(2)}) copy-start(bf16[24,8,8,128]{3,2,1,0:T(8,128)(2,1)S(1)} %copy.33) | copy-start | bytes 1179652
  17.7 7.3 %collective-permute-start.1 = (bf16[32,2048]{1,0:T(8,128)(2,1)S(1)}, bf16[32,2048]{1,0:T(8,128)(2,1)S(1)}, u32[]{:S(2)}, u32[]{:S(2)}) collective-permute-start(bf16[32,2048]{1,0:T(8,128)(2,1)S(1)} %broadcast_select_fusion.5), channel_id=1, source_target_pairs={{0,12},{6,18},{12,0},{18,6},{24,36},{30,42},{36,24},{42,30},{48,60... | collective-permute-start | bytes 393224 | tf_op jit(solution)/shard_map/ppermute | solution.py:10
  25.0 15.0 %collective-permute-start.2 = (bf16[32,2048]{1,0:T(8,128)(2,1)S(1)}, bf16[32,2048]{1,0:T(8,128)(2,1)S(1)}, u32[]{:S(2)}, u32[]{:S(2)}) collective-permute-start(bf16[32,2048]{1,0:T(8,128)(2,1)S(1)} %broadcast_select_fusion.7), channel_id=1, source_target_pairs={{0,24},{6,30},{12,36},{18,42},{24,0},{30,6},{36,12},{42,18},{48,72... | collective-permute-start | bytes 393224 | tf_op jit(solution)/shard_map/ppermute | solution.py:10
  36.5 12.2 %collective-permute-start.4 = (bf16[192,1024]{1,0:T(8,128)(2,1)S(1)}, bf16[192,1024]{1,0:T(8,128)(2,1)S(1)}, u32[]{:S(2)}, u32[]{:S(2)}) collective-permute-start(bf16[192,1024]{1,0:T(8,128)(2,1)S(1)} %broadcast_select_fusion.1), channel_id=1, source_target_pairs={{0,12},{6,18},{12,0},{18,6},{24,36},{30,42},{36,24},{42,30},{48,60... | collective-permute-start | bytes 1179656 | tf_op jit(solution)/shard_map/ppermute | solution.py:10
  48.7 36.0 %copy-start.7 = (bf16[192,1024]{1,0:T(8,128)(2,1)}, bf16[192,1024]{1,0:T(8,128)(2,1)S(1)}, u32[]{:S(2)}) copy-start(bf16[192,1024]{1,0:T(8,128)(2,1)S(1)} %broadcast_select_fusion.3) | copy-start | bytes 1179652
  48.7 35.6 %collective-permute-start.5 = (bf16[192,1024]{1,0:T(8,128)(2,1)S(1)}, bf16[192,1024]{1,0:T(8,128)(2,1)S(1)}, u32[]{:S(2)}, u32[]{:S(2)}) collective-permute-start(bf16[192,1024]{1,0:T(8,128)(2,1)S(1)} %broadcast_select_fusion.3), channel_id=1, source_target_pairs={{0,24},{6,30},{12,36},{18,42},{24,0},{30,6},{36,12},{42,18},{48,72... | collective-permute-start | bytes 1179656 | tf_op jit(solution)/shard_map/ppermute | solution.py:10
  84.3 0.8 copy-start.3
  84.3 0.9 copy-start.10
  87.3 1.7 copy-start.1
  87.3 1.7 copy-start.5
  89.0 1.0 copy-start.8
  89.0 1.1 copy-start.11
  90.1 1.0 copy-start.2
  90.8 1.3 copy-start.4
  92.9 51.1 %collective-permute-start.6 = (bf16[192,1024]{1,0:T(8,128)(2,1)S(1)}, bf16[192,1024]{1,0:T(8,128)(2,1)S(1)}, u32[]{:S(2)}, u32[]{:S(2)}) collective-permute-start(bf16[192,1024]{1,0:T(8,128)(2,1)S(1)} %bitcast.116), channel_id=1, source_target_pairs={{0,6},{6,0},{12,18},{18,12},{24,30},{30,24},{36,42},{42,36},{48,54... | collective-permute-start | bytes 1179656 | tf_op jit(solution)/shard_map/ppermute | solution.py:10
  142.1 4.9 %collective-permute-start.9 = (bf16[32,2048]{1,0:T(8,128)(2,1)}, bf16[32,2048]{1,0:T(8,128)(2,1)S(1)}, u32[]{:S(2)}, u32[]{:S(2)}) collective-permute-start(bf16[32,2048]{1,0:T(8,128)(2,1)} %bitcast.119), channel_id=1, source_target_pairs={{0,6},{6,0},{12,18},{18,12},{24,30},{30,24},{36,42},{42,36},{48,54... | collective-permute-start | bytes 393224 | tf_op jit(solution)/shard_map/ppermute | solution.py:10
  144.1 13.8 %collective-permute-start.7 = (bf16[192,1024]{1,0:T(8,128)(2,1)S(1)}, bf16[192,1024]{1,0:T(8,128)(2,1)S(1)}, u32[]{:S(2)}, u32[]{:S(2)}) collective-permute-start(bf16[192,1024]{1,0:T(8,128)(2,1)S(1)} %broadcast_select_fusion), channel_id=1, source_target_pairs={{0,12},{6,18},{12,0},{18,6},{24,36},{30,42},{36,24},{42,30},{48,60... | collective-permute-start | bytes 1179656 | tf_op jit(solution)/shard_map/ppermute | solution.py:10
  147.9 12.4 %collective-permute-start.10 = (bf16[32,2048]{1,0:T(8,128)(2,1)S(1)}, bf16[32,2048]{1,0:T(8,128)(2,1)S(1)}, u32[]{:S(2)}, u32[]{:S(2)}) collective-permute-start(bf16[32,2048]{1,0:T(8,128)(2,1)S(1)} %broadcast_select_fusion.4), channel_id=1, source_target_pairs={{0,12},{6,18},{12,0},{18,6},{24,36},{30,42},{36,24},{42,30},{48,60... | collective-permute-start | bytes 393224 | tf_op jit(solution)/shard_map/ppermute | solution.py:10
  157.9 15.1 %collective-permute-start.8 = (bf16[192,1024]{1,0:T(8,128)(2,1)S(1)}, bf16[192,1024]{1,0:T(8,128)(2,1)S(1)}, u32[]{:S(2)}, u32[]{:S(2)}) collective-permute-start(bf16[192,1024]{1,0:T(8,128)(2,1)S(1)} %broadcast_select_fusion.2), channel_id=1, source_target_pairs={{0,24},{6,30},{12,36},{18,42},{24,0},{30,6},{36,12},{42,18},{48,72... | collective-permute-start | bytes 1179656 | tf_op jit(solution)/shard_map/ppermute | solution.py:10
  160.4 14.1 %collective-permute-start.11 = (bf16[32,2048]{1,0:T(8,128)(2,1)S(1)}, bf16[32,2048]{1,0:T(8,128)(2,1)S(1)}, u32[]{:S(2)}, u32[]{:S(2)}) collective-permute-start(bf16[32,2048]{1,0:T(8,128)(2,1)S(1)} %broadcast_select_fusion.6), channel_id=1, source_target_pairs={{0,24},{6,30},{12,36},{18,42},{24,0},{30,6},{36,12},{42,18},{48,72... | collective-permute-start | bytes 393224 | tf_op jit(solution)/shard_map/ppermute | solution.py:10
Sparse Core Ops, SparseCore 0:
  92.2 49.8 reduce-scatter.1
where the time goes:
time: 183 us; the launch traced here: 182 us
  waiting for transfers between devices  76 us (42%)
  starting transfers between devices  40.6 us (22%)
  blocking collectives  32.8 us (18%)
  between operations  15.8 us (9%)
  other arithmetic  7.41 us (4%)
  local copies, waits for them, and re-layouts  5.37 us (3%)
  matrix products  3.89 us (2%)
    reduce_scatter x1, waiting for transfers between devices, attend(): lax.psum_scatter(terms.astype(jnp.bfloat16), 'tensor', scatter_dimension=...  47.2 us
    ppermute x12, starting transfers between devices, from_partner(): lax.ppermute(x, axis, [(i, i ^ 1 << apart) for i in range(lax.axis_size(a...  40.6 us
    all_gather x1, blocking collectives, attend(): gathered = lax.all_gather(keyval, 'tensor', axis=0, tiled=True)  32.8 us
    ppermute x12, waiting for transfers between devices, from_partner(): lax.ppermute(x, axis, [(i, i ^ 1 << apart) for i in range(lax.axis_size(a...  28.8 us
  transfers between devices with their start and end apart: 13, of which 7 were waited for; matrix products, arithmetic and copies ran while one was open for 5% of the time, Pallas kernels for 0%

commit v1 on v0

v1 whole, which is shorter than its diff:
```python
import functools

import jax
import jax.numpy as jnp
from jax import lax
from jax.experimental import pallas as pl
from jax.experimental.pallas import tpu as pltpu
from jax.sharding import PartitionSpec as P

HEAD_DIM = 128
MESH = pl.DeviceIdType.MESH
NT = (((1,), (1,)), ((), ()))
NN = (((1,), (0,)), ((), ()))
TN = (((0,), (0,)), ((), ()))


def dot(a, b, dims):
    return lax.dot_general(a, b, dims, preferred_element_type=jnp.float32)


def kernel(
    nt, nh,
    len_ref, route_ref, adv_ref, q_hbm, kv_hbm, cot_hbm, dq_hbm, dkv_hbm,
    q, cot, kvin, kvb, g0, gsib, sel1, ga, sela, gb, part, upb, dnb, dqb, dkvb,
    in_sem, dq_sem, dkv_sem,
    kv_r, kv_su, kv_sd, ru_r, ru_s, rd_r, rd_s,
    sib_s, sib_r, a_s, a_r, b_s, b_r,
):
    dp = lax.axis_index("dp")
    t = lax.axis_index("tensor")
    slot = q.shape[0]
    rows = slot // nt
    kvw = nh * HEAD_DIM
    last = nt - 1
    core = lax.rem(dp, 2)
    x = lax.rem(lax.div(dp, 2), 4)
    sib = dp + 1 - 2 * core
    near_a = dp + 2 * (1 - 2 * lax.rem(x, 2))
    near_b = dp + 2 * (3 - 2 * x)
    up = jnp.minimum(t + 1, last)
    down = jnp.maximum(t - 1, 0)
    scale = 1.0 / HEAD_DIM**0.5

    load_kv = pltpu.make_async_copy(kv_hbm, kvin, in_sem.at[0])
    load_cot = pltpu.make_async_copy(cot_hbm, cot, in_sem.at[1])
    load_q = pltpu.make_async_copy(q_hbm, q, in_sem.at[2])
    load_kv.start()
    load_cot.start()
    load_q.start()

    barrier = pltpu.get_barrier_semaphore()

    def greet(where, index):
        pl.semaphore_signal(barrier, inc=1, device_id=(where, index), device_id_type=MESH)

    greet(sib, t)
    greet(near_a, t)
    greet(near_b, t)

    @pl.when(t < last)
    def _():
        greet(dp, up)

    @pl.when(t > 0)
    def _():
        greet(dp, down)

    def remote(src, dst, send, recv, where, index):
        return pltpu.make_async_remote_copy(
            src_ref=src, dst_ref=dst, send_sem=send, recv_sem=recv, device_id=(where, index), device_id_type=MESH
        )

    def band(s):
        return pl.ds(pl.multiple_of(s * rows, rows), rows)

    def kv_up(s, h):
        block = kvb.at[h, band(s)]
        return remote(block, block, kv_su.at[s, h], kv_r.at[s, h], dp, up)

    def kv_down(s, h):
        block = kvb.at[h, band(s)]
        return remote(block, block, kv_sd.at[s, h], kv_r.at[s, h], dp, down)

    def sum_up(src, s, h):
        return remote(src.at[h, band(s)], upb.at[h, band(s)], ru_s.at[s, h], ru_r.at[s, h], dp, up)

    def sum_down(src, s, h):
        return remote(src.at[h, band(s)], dnb.at[h, band(s)], rd_s.at[s, h], rd_r.at[s, h], dp, down)

    def to_sib(h):
        return remote(g0.at[h], gsib.at[h], sib_s.at[h], sib_r.at[h], sib, t)

    def to_a(h):
        return remote(sel1.at[h], ga.at[h], a_s.at[h], a_r.at[h], near_a, t)

    def to_b(h):
        return remote(sela.at[h], gb.at[h], b_s.at[h], b_r.at[h], near_b, t)

    def head(h):
        return pl.ds(pl.multiple_of(h * HEAD_DIM, HEAD_DIM), HEAD_DIM)

    def value_head(h):
        return pl.ds(pl.multiple_of(kvw + h * HEAD_DIM, HEAD_DIM), HEAD_DIM)

    load_kv.wait()

    @pl.loop(0, nh)
    def _(h):
        kvb[h, band(t), 0:HEAD_DIM] = kvin[:, head(h)]
        kvb[h, band(t), HEAD_DIM : 2 * HEAD_DIM] = kvin[:, value_head(h)]

    pl.semaphore_wait(barrier, 3 + (t > 0).astype(jnp.int32) + (t < last).astype(jnp.int32))

    @pl.loop(0, nh)
    def _(h):
        @pl.when(t < last)
        def _():
            kv_up(t, h).start()

        @pl.when(t > 0)
        def _():
            kv_down(t, h).start()

    code = route_ref[0]
    moved = jnp.bitwise_xor(dp, code)
    slot_len = len_ref[moved]
    factor = slot / jnp.full((1, slot), slot_len, jnp.int32).astype(jnp.float32)
    place = lax.broadcasted_iota(jnp.int32, (1, slot), 1)
    live = (place < slot_len).astype(jnp.float32)
    weight = adv_ref[...].astype(jnp.float32) / 256.0 * factor * live
    weight = jnp.broadcast_to(weight, (HEAD_DIM, slot)).T
    load_cot.wait()

    @pl.loop(0, nh)
    def _(h):
        g0[h] = (cot[:, head(h)].astype(jnp.float32) * weight).astype(jnp.bfloat16)
        to_sib(h).start()

    x_code = jnp.bitwise_and(lax.shift_right_logical(code, 1), 3)
    use_sib = jnp.full((1, HEAD_DIM), jnp.bitwise_and(code, 1), jnp.int32) == 1
    x_full = jnp.full((1, HEAD_DIM), x_code, jnp.int32)
    use_a = jnp.logical_or(x_full == 1, x_full == 2)
    use_b = x_full >= 2

    @pl.loop(0, nh)
    def _(h):
        to_sib(h).wait_recv()
        sel1[h] = jnp.where(use_sib, gsib[h], g0[h])
        to_a(h).start()

    def hop_b(h):
        to_a(h).wait_recv()
        sela[h] = jnp.where(use_a, ga[h], sel1[h])
        to_b(h).start()

    def gather(h):
        for d in range(1, nt):
            s_lo = t - d
            s_hi = t + d

            @pl.when(s_lo >= 0)
            def _():
                kv_up(s_lo, h).wait_recv()

                @pl.when(t < last)
                def _():
                    kv_up(s_lo, h).start()

            @pl.when(s_hi <= last)
            def _():
                kv_down(s_hi, h).wait_recv()

                @pl.when(t > 0)
                def _():
                    kv_down(s_hi, h).start()

    home_len = len_ref[dp]
    key_at = lax.broadcasted_iota(jnp.int32, (slot, slot), 0)
    query_at = lax.broadcasted_iota(jnp.int32, (slot, slot), 1)

    def compute(h):
        to_b(h).wait_recv()
        grad = jnp.where(use_b, gb[h], sela[h])
        query = q[:, head(h)]
        key = kvb[h, :, 0:HEAD_DIM]
        value = kvb[h, :, HEAD_DIM : 2 * HEAD_DIM]
        allowed = jnp.logical_and(key_at <= query_at, key_at < home_len)
        scores = dot(key, query, NT) * scale
        dprob = dot(value, grad, NT)
        scores = jnp.where(allowed, scores, -1e30)
        expo = jnp.exp(scores - jnp.max(scores, axis=0, keepdims=True))
        probs = expo * (1.0 / jnp.sum(expo, axis=0, keepdims=True))
        probs_b = probs.astype(jnp.bfloat16)
        delta = jnp.sum(probs_b.astype(jnp.float32) * dprob, axis=0, keepdims=True)
        dscore = (probs * (dprob - delta)).astype(jnp.bfloat16)
        part[h, :, 0:HEAD_DIM] = (dot(dscore, query, NN) * scale).astype(jnp.bfloat16)
        part[h, :, HEAD_DIM : 2 * HEAD_DIM] = dot(probs_b, grad, NN).astype(jnp.bfloat16)

        @pl.when(t == 0)
        def _():
            for s in range(last, 0, -1):
                sum_up(part, s, h).start()

        @pl.when(t == last)
        def _():
            for s in range(last):
                sum_down(part, s, h).start()

        dqb[:, head(h)] = (dot(dscore, key, TN) * scale).astype(jnp.bfloat16)
        store_dq(h).start()

    def store_dq(h):
        return pltpu.make_async_copy(dqb.at[:, head(h)], dq_hbm.at[:, head(h)], dq_sem.at[h])

    def add(buf, s, h):
        total = buf[h, band(s)].astype(jnp.float32) + part[h, band(s)].astype(jnp.float32)
        buf[h, band(s)] = total.astype(jnp.bfloat16)

    def relay_up(h):
        for s in range(last, 1, -1):

            @pl.when(t < s)
            def _():
                sum_up(upb, s, h).wait_recv()
                add(upb, s, h)
                sum_up(upb, s, h).start()

    def relay_down(h):
        for s in range(last - 1):

            @pl.when(t > s)
            def _():
                sum_down(dnb, s, h).wait_recv()
                add(dnb, s, h)
                sum_down(dnb, s, h).start()

    def finish(h):
        @pl.when(t > 0)
        def _():
            sum_up(upb, t, h).wait_recv()

        @pl.when(t < last)
        def _():
            sum_down(dnb, t, h).wait_recv()

        has_up = jnp.full((1, 2 * HEAD_DIM), t, jnp.int32) > 0
        has_down = jnp.full((1, 2 * HEAD_DIM), t, jnp.int32) < last
        total = part[h, band(t)].astype(jnp.float32)
        total += jnp.where(has_up, upb[h, band(t)].astype(jnp.float32), 0.0)
        total += jnp.where(has_down, dnb[h, band(t)].astype(jnp.float32), 0.0)
        total = total.astype(jnp.bfloat16)
        dkvb[:, head(h)] = total[:, 0:HEAD_DIM]
        dkvb[:, value_head(h)] = total[:, HEAD_DIM:]

    hop_b(0)
    load_q.wait()

    @pl.loop(0, nh + last)
    def _(n):
        @pl.when(n + 1 < nh)
        def _():
            hop_b(n + 1)

        @pl.when(n < nh)
        def _():
            gather(n)
            compute(n)

        h_up = n - t
        h_down = n - (last - t)

        @pl.when(jnp.logical_and(t > 0, jnp.logical_and(h_up >= 0, h_up < nh)))
        def _():
            relay_up(h_up)

        @pl.when(jnp.logical_and(t < last, jnp.logical_and(h_down >= 0, h_down < nh)))
        def _():
            relay_down(h_down)

        @pl.when(n >= last)
        def _():
            finish(n - last)

    store_dkv = pltpu.make_async_copy(dkvb, dkv_hbm, dkv_sem)
    store_dkv.start()

    @pl.loop(0, nh)
    def _(h):
        to_sib(h).wait_send()
        to_a(h).wait_send()
        to_b(h).wait_send()
        store_dq(h).wait()
        for s in range(nt):

            @pl.when(jnp.logical_and(t < last, s <= t))
            def _():
                kv_up(s, h).wait_send()

            @pl.when(jnp.logical_and(t > 0, s >= t))
            def _():
                kv_down(s, h).wait_send()

            @pl.when(s > t)
            def _():
                sum_up(upb, s, h).wait_send()

            @pl.when(s < t)
            def _():
                sum_down(dnb, s, h).wait_send()

    store_dkv.wait()


def on_device(queries, keys_values, lengths, route, cotangent, advantage):
    slot, _, qwidth = queries.shape
    rows, _, kv2 = keys_values.shape
    nt = lax.axis_size("tensor")
    nh = kv2 // 2 // HEAD_DIM
    wide = 2 * HEAD_DIM
    bf16 = jnp.bfloat16
    heads = pltpu.VMEM((nh, slot, HEAD_DIM), bf16)
    blocks = pltpu.VMEM((nh, slot, wide), bf16)
    dma = pltpu.SemaphoreType.DMA
    dq, dkv = pl.pallas_call(
        functools.partial(kernel, nt, nh),
        out_shape=(
            jax.ShapeDtypeStruct((slot, qwidth), bf16),
            jax.ShapeDtypeStruct((rows, kv2), bf16),
        ),
        in_specs=[
            pl.BlockSpec(memory_space=pltpu.SMEM),
            pl.BlockSpec(memory_space=pltpu.SMEM),
            pl.BlockSpec(memory_space=pltpu.VMEM),
            pl.BlockSpec(memory_space=pl.ANY),
            pl.BlockSpec(memory_space=pl.ANY),
            pl.BlockSpec(memory_space=pl.ANY),
        ],
        out_specs=(pl.BlockSpec(memory_space=pl.ANY), pl.BlockSpec(memory_space=pl.ANY)),
        scratch_shapes=[
            pltpu.VMEM((slot, qwidth), bf16),
            pltpu.VMEM((slot, qwidth), bf16),
            pltpu.VMEM((rows, kv2), bf16),
            blocks,
            heads, heads, heads, heads, heads, heads,
            blocks, blocks, blocks,
            pltpu.VMEM((slot, qwidth), bf16),
            pltpu.VMEM((rows, kv2), bf16),
            dma((3,)), dma((nh,)), dma,
            dma((nt, nh)), dma((nt, nh)), dma((nt, nh)),
            dma((nt, nh)), dma((nt, nh)), dma((nt, nh)), dma((nt, nh)),
            dma((nh,)), dma((nh,)), dma((nh,)), dma((nh,)), dma((nh,)), dma((nh,)),
        ],
        compiler_params=pltpu.CompilerParams(
            collective_id=0, has_side_effects=True, vmem_limit_bytes=60 * 1024 * 1024
        ),
        name="attention_grads",
    )(
        lengths,
        route,
        advantage.reshape(1, slot),
        queries.reshape(slot, qwidth),
        keys_values.reshape(rows, kv2),
        cotangent.reshape(slot, qwidth),
    )
    return dq.reshape(slot, 1, qwidth), dkv.reshape(rows, 1, kv2)


def solution(mesh):
    placed = (
        P(None, "dp", "tensor"),
        P("tensor", "dp", None),
        P(),
        P(),
        P(None, "dp", "tensor"),
        P(None, "dp"),
    )
    return jax.shard_map(
        on_device,
        mesh=mesh,
        in_specs=placed,
        out_specs=(P(None, "dp", "tensor"), P("tensor", "dp", None)),
        check_vma=False,
    )
```

time: 183 us -> 121 us (0.66)
  the two profiles are of different devices: /device:TPU:4 before, /device:TPU:8 now
where the time goes in v1:
time: 121 us
  Pallas kernels  117 us (97%)
  local copies, waits for them, and re-layouts  2.46 us (2%)
  between operations  1.29 us (1%)
    pallas_call x1, Pallas kernels, on_device(): pl.pallas_call(functools.partial(kernel, nt, nh), out_shape=(jax.ShapeDty...  117 us
    unnamed x4, local copies, waits for them, and re-layouts  2.46 us

profile of v1, /device:TPU:8, one launch (start us, length us, event | category | flops | bytes accessed | tf_op | source)
XLA Modules:
  0.0 120.5 jit_solution(14277202599638780175)
XLA Ops:
  1.3 116.8 %attention_grads.1 = (bf16[192,1024]{1,0:T(8,128)(2,1)}, bf16[32,2048]{1,0:T(8,128)(2,1)}) custom-call(s32[128]{0:T(128)} %len_ref.1, s32[1]{0:T(128)S(6)} %copy.10.route_ref, s32[1,192]{1,0:T(1,128)} %bitcast.11, bf16[192,1024]{1,0:T(8,128)(2,1)} %bitcast.6, bf16[32,2048]{1,0:T(8,128)(2,1)} %bitcast.9, bf16[192,1024]{1,0:T(8,128)(2,1)} %bitcast.7), custom_call_target="tpu_custom_call" | custom-call | tf_op jit(solution)/shard_map/attention_grads/pallas_call | solution.py:324
  118.1 0.0 copy-start
  118.1 1.8 %copy.11 = bf16[192,1,1024]{2,0,1:T(8,128)(2,1)} copy(bf16[192,1,1024]{2,0,1:T(8,128)(2,1)} %bitcast.8) | data formatting | bytes 786432
  119.9 0.0 copy-done
  119.9 0.7 copy.12
Async XLA Ops:
  118.1 1.8 %copy-start = (bf16[32,2048]{1,0:T(8,128)(2,1)S(1)}, bf16[32,2048]{1,0:T(8,128)(2,1)}, u32[]{:S(2)}) copy-start(bf16[32,2048]{1,0:T(8,128)(2,1)} %get-tuple-element.5) | copy-start | bytes 393220

commit v2 on v0

v2 whole, which is shorter than its diff:
```python
import functools

import jax
import jax.numpy as jnp
from jax import lax
from jax.experimental import pallas as pl
from jax.experimental.pallas import tpu as pltpu
from jax.sharding import PartitionSpec as P

HEAD_DIM = 128
MESH = pl.DeviceIdType.MESH
NT = (((1,), (1,)), ((), ()))
NN = (((1,), (0,)), ((), ()))
TN = (((0,), (0,)), ((), ()))


def dot(a, b, dims):
    return lax.dot_general(a, b, dims, preferred_element_type=jnp.float32)


LINE = 6
HEADS = (1, 2, 2, 2, 1)
AHEAD = 1
ISSUED = 2
RELAY_LAG = 1
FINISH_LAG = 2

TWO_STOPS = ((0, 1, 0, 3, 3), (1, 2, 1, 4), (2, 2, 4), (3, 4), (4,))
KV_TREES = (TWO_STOPS,) * len(HEADS)
SUM_TREES = (TWO_STOPS,) * len(HEADS)


def plan(tree):
    copies = []
    for s, parents in enumerate(tree):
        for i, a in enumerate(parents):
            b = s + 1 + i
            copies.append((s, a, b))
            copies.append((LINE - 1 - s, LINE - 1 - a, LINE - 1 - b))
    copies.sort(key=lambda c: (abs(c[0] - c[1]), -abs(c[0] - c[2]), c))
    used = [0] * LINE
    edges = []
    for s, a, b in copies:
        edges.append((s, a, b, used[a]))
        used[a] += 1
    return edges


def outgoing(edges, s, a):
    return [e for e in edges if e[0] == s and e[1] == a]


def stops(edges):
    return sorted({(s, a) for s, a, _, _ in edges if s != a}, key=lambda c: (abs(c[0] - c[1]), c))


STEPS = len(HEADS)
FIRST = [sum(HEADS[:n]) for n in range(STEPS)]
KV_EDGES = [plan(tree) for tree in KV_TREES]
SUM_EDGES = [plan(tree) for tree in SUM_TREES]
KV_SLOTS = 1 + max(e[3] for edges in KV_EDGES for e in edges)
SUM_SLOTS = [1 + max(e[3] for e in edges) for edges in SUM_EDGES]
PARTNERS = {frozenset((e[1], e[2])) for edges in KV_EDGES + SUM_EDGES for e in edges}


def one_of(t, members):
    found = t == members[0]
    for m in members[1:]:
        found = jnp.logical_or(found, t == m)
    return found


def kernel(nt, nh, len_ref, route_ref, adv_ref, q_hbm, kv_hbm, cot_hbm, dq_hbm, dkv_hbm, *scratch):
    scratch = list(scratch)

    def take(count):
        taken = scratch[:count]
        del scratch[:count]
        return taken

    q, cot, dqb, dkvb = take(4)
    kvb, part, sums, arrived = take(STEPS), take(STEPS), take(STEPS), take(STEPS)
    g0, gsib, sel1, ga, sela, gb = [take(STEPS) for _ in range(6)]
    in_sem, own_sem, dq_sem, dkv_sem = take(4)
    kv_r, kv_s, sum_r, sum_s = take(4)
    sib_s, sib_r, a_s, a_r, b_s, b_r = take(6)

    dp = lax.axis_index("dp")
    t = lax.axis_index("tensor")
    slot = q.shape[0]
    rows = slot // nt
    kvw = nh * HEAD_DIM
    core = lax.rem(dp, 2)
    x = lax.rem(lax.div(dp, 2), 4)
    sib = dp + 1 - 2 * core
    near_a = dp + 2 * (1 - 2 * lax.rem(x, 2))
    near_b = dp + 2 * (3 - 2 * x)
    scale = 1.0 / HEAD_DIM**0.5

    barrier = pltpu.get_barrier_semaphore()

    def greet(where, index):
        pl.semaphore_signal(barrier, inc=1, device_id=(where, index), device_id_type=MESH)

    greet(sib, t)
    greet(near_a, t)
    greet(near_b, t)
    greetings = 3
    for s in range(nt):
        met = [m for m in range(nt) if frozenset((m, s)) in PARTNERS]

        @pl.when(one_of(t, met))
        def _():
            greet(dp, s)

        greetings += one_of(t, met).astype(jnp.int32)

    def remote(src, dst, send, recv, where, index):
        return pltpu.make_async_remote_copy(
            src_ref=src, dst_ref=dst, send_sem=send, recv_sem=recv, device_id=(where, index), device_id_type=MESH
        )

    def band(s):
        return pl.ds(pl.multiple_of(s * rows, rows), rows)

    def columns(n, start=0):
        return pl.ds(start + FIRST[n] * HEAD_DIM, HEADS[n] * HEAD_DIM)

    def halves(n):
        group = HEADS[n] * HEAD_DIM
        return ((columns(n), pl.ds(0, group)), (columns(n, kvw), pl.ds(group, group)))

    def own(n):
        block = kvb[n].at[band(t)]
        return pltpu.make_async_copy(block, block, own_sem.at[n])

    def kv_copy(edge, n):
        s, _, b, k = edge
        block = kvb[n].at[band(s)]
        return remote(block, block, kv_s.at[k, n], kv_r.at[s, n], dp, b)

    def kv_arrival(s, n):
        block = kvb[n].at[band(s)]
        return remote(block, block, kv_s.at[0, n], kv_r.at[s, n], dp, t)

    def sum_copy(src, edge, n):
        s, a, _, k = edge
        return remote(src[n].at[band(s)], arrived[n].at[k], sum_s.at[s, n], sum_r.at[k, n], dp, a)

    def to_sib(n):
        return remote(g0[n], gsib[n], sib_s.at[n], sib_r.at[n], sib, t)

    def to_a(n):
        return remote(sel1[n], ga[n], a_s.at[n], a_r.at[n], near_a, t)

    def to_b(n):
        return remote(sela[n], gb[n], b_s.at[n], b_r.at[n], near_b, t)

    def load_own(n):
        for there, here in halves(n):
            pltpu.make_async_copy(kv_hbm.at[:, there], kvb[n].at[band(t), here], own_sem.at[n]).start()

    def direct(n):
        for edge in KV_EDGES[n]:
            s, a, b, k = edge
            if s == a:

                @pl.when(t == a)
                def _():
                    for there, here in halves(n):
                        remote(
                            kv_hbm.at[:, there], kvb[n].at[band(s), here], kv_s.at[k, n], kv_r.at[s, n], dp, b
                        ).start()

    def relay(n):
        for s, a in stops(KV_EDGES[n]):

            @pl.when(t == a)
            def _():
                kv_arrival(s, n).wait_recv()
                for edge in outgoing(KV_EDGES[n], s, a):
                    kv_copy(edge, n).start()

    def arrive(n):
        own(n).wait()
        for s in range(nt):
            leaves = [m for m in range(nt) if m != s and not outgoing(KV_EDGES[n], s, m)]

            @pl.when(one_of(t, leaves))
            def _():
                kv_arrival(s, n).wait_recv()

    load_cot = pltpu.make_async_copy(cot_hbm, cot, in_sem.at[0])
    load_q = pltpu.make_async_copy(q_hbm, q, in_sem.at[1])
    load_cot.start()
    pl.semaphore_wait(barrier, greetings)
    for n in range(min(ISSUED, STEPS)):
        direct(n)
    for n in range(STEPS):
        load_own(n)
    load_q.start()

    code = route_ref[0]
    moved = jnp.bitwise_xor(dp, code)
    slot_len = len_ref[moved]
    factor = slot / jnp.full((1, slot), slot_len, jnp.int32).astype(jnp.float32)
    place = lax.broadcasted_iota(jnp.int32, (1, slot), 1)
    live = (place < slot_len).astype(jnp.float32)
    weight = adv_ref[...].astype(jnp.float32) / 256.0 * factor * live
    weight = jnp.broadcast_to(weight, (HEAD_DIM, slot)).T
    load_cot.wait()
    for n in range(STEPS):
        wide = jnp.concatenate([weight] * HEADS[n], axis=1)
        g0[n][...] = (cot[:, columns(n)].astype(jnp.float32) * wide).astype(jnp.bfloat16)
        to_sib(n).start()

    x_code = jnp.bitwise_and(lax.shift_right_logical(code, 1), 3)

    def chosen(n, flag):
        return jnp.full((1, HEADS[n] * HEAD_DIM), flag, jnp.int32) == 1

    use_sib = jnp.bitwise_and(code, 1)
    use_a = jnp.logical_or(x_code == 1, x_code == 2).astype(jnp.int32)
    use_b = (x_code >= 2).astype(jnp.int32)

    for n in range(STEPS):
        to_sib(n).wait_recv()
        sel1[n][...] = jnp.where(chosen(n, use_sib), gsib[n][...], g0[n][...])
        to_a(n).start()

    def hop_b(n):
        to_a(n).wait_recv()
        sela[n][...] = jnp.where(chosen(n, use_a), ga[n][...], sel1[n][...])
        to_b(n).start()

    home_len = len_ref[dp]
    key_at = lax.broadcasted_iota(jnp.int32, (slot, slot), 0)
    query_at = lax.broadcasted_iota(jnp.int32, (slot, slot), 1)

    def one_head(n, j, grad):
        here = pl.ds(j * HEAD_DIM, HEAD_DIM)
        there = pl.ds((HEADS[n] + j) * HEAD_DIM, HEAD_DIM)
        at = pl.ds((FIRST[n] + j) * HEAD_DIM, HEAD_DIM)
        query = q[:, at]
        key = kvb[n][:, here]
        value = kvb[n][:, there]
        allowed = jnp.logical_and(key_at <= query_at, key_at < home_len)
        scores = dot(key, query, NT) * scale
        dprob = dot(value, grad, NT)
        scores = jnp.where(allowed, scores, -1e30)
        expo = jnp.exp(scores - jnp.max(scores, axis=0, keepdims=True))
        probs = expo * (1.0 / jnp.sum(expo, axis=0, keepdims=True))
        probs_b = probs.astype(jnp.bfloat16)
        delta = jnp.sum(probs_b.astype(jnp.float32) * dprob, axis=0, keepdims=True)
        dscore = (probs * (dprob - delta)).astype(jnp.bfloat16)
        part[n][:, here] = (dot(dscore, query, NN) * scale).astype(jnp.bfloat16)
        part[n][:, there] = dot(probs_b, grad, NN).astype(jnp.bfloat16)
        dqb[:, at] = (dot(dscore, key, TN) * scale).astype(jnp.bfloat16)

    def compute(n):
        to_b(n).wait_recv()
        grad = jnp.where(chosen(n, use_b), gb[n][...], sela[n][...])
        for j in range(HEADS[n]):
            one_head(n, j, grad[:, j * HEAD_DIM : (j + 1) * HEAD_DIM])
        for edge in SUM_EDGES[n]:
            if not outgoing(SUM_EDGES[n], edge[0], edge[2]):

                @pl.when(t == edge[2])
                def _():
                    sum_copy(part, edge, n).start()

        store_dq(n).start()

    def store_dq(n):
        return pltpu.make_async_copy(dqb.at[:, columns(n)], dq_hbm.at[:, columns(n)], dq_sem.at[n])

    def collect(s, a, n):
        total = part[n][band(s)].astype(jnp.float32)
        for edge in outgoing(SUM_EDGES[n], s, a):
            sum_copy(sums, edge, n).wait_recv()
            total += arrived[n][edge[3]].astype(jnp.float32)
        return total.astype(jnp.bfloat16)

    def relay_sums(n):
        for s, a in reversed(stops(SUM_EDGES[n])):
            into = [e for e in SUM_EDGES[n] if e[0] == s and e[2] == a][0]

            @pl.when(t == a)
            def _():
                sums[n][band(s)] = collect(s, a, n)
                sum_copy(sums, into, n).start()

    def store_dkv(n, half):
        there = halves(n)[half][0]
        return pltpu.make_async_copy(dkvb.at[:, there], dkv_hbm.at[:, there], dkv_sem.at[n, half])

    def finish(n):
        group = HEADS[n] * HEAD_DIM
        for s in range(nt):

            @pl.when(t == s)
            def _():
                total = collect(s, s, n)
                dkvb[:, columns(n)] = total[:, 0:group]
                dkvb[:, columns(n, kvw)] = total[:, group:]

        store_dkv(n, 0).start()
        store_dkv(n, 1).start()

    def sums_sent(n):
        for edge in SUM_EDGES[n]:

            @pl.when(t == edge[2])
            def _():
                sum_copy(sums, edge, n).wait_send()

    def sent(n):
        to_sib(n).wait_send()
        to_a(n).wait_send()
        to_b(n).wait_send()
        store_dq(n).wait()
        for edge in KV_EDGES[n]:

            @pl.when(t == edge[1])
            def _():
                kv_copy(edge, n).wait_send()

    for n in range(AHEAD):
        relay(n)
    hop_b(0)
    load_q.wait()

    for n in range(STEPS + FINISH_LAG):
        if n + ISSUED < STEPS:
            direct(n + ISSUED)
        if n + AHEAD < STEPS:
            relay(n + AHEAD)
        if n + 1 < STEPS:
            hop_b(n + 1)
        if n < STEPS:
            arrive(n)
            compute(n)
        if RELAY_LAG <= n < STEPS + RELAY_LAG:
            relay_sums(n - RELAY_LAG)
        if n == STEPS + RELAY_LAG - 1:
            for m in range(STEPS):
                sent(m)
            for m in range(STEPS - 1):
                sums_sent(m)
        if n >= FINISH_LAG:
            finish(n - FINISH_LAG)

    sums_sent(STEPS - 1)
    for n in range(STEPS):
        store_dkv(n, 0).wait()
        store_dkv(n, 1).wait()


def on_device(queries, keys_values, lengths, route, cotangent, advantage):
    slot, _, qwidth = queries.shape
    rows, _, kv2 = keys_values.shape
    nt = lax.axis_size("tensor")
    nh = kv2 // 2 // HEAD_DIM
    bf16 = jnp.bfloat16
    dma = pltpu.SemaphoreType.DMA
    smem = pl.BlockSpec(memory_space=pltpu.SMEM)
    hbm = pl.BlockSpec(memory_space=pl.ANY)
    width = [h * HEAD_DIM for h in HEADS]
    blocks = [pltpu.VMEM((slot, 2 * w), bf16) for w in width]
    grads = [pltpu.VMEM((slot, w), bf16) for w in width]
    dq, dkv = pl.pallas_call(
        functools.partial(kernel, nt, nh),
        out_shape=(
            jax.ShapeDtypeStruct((slot, qwidth), bf16),
            jax.ShapeDtypeStruct((rows, kv2), bf16),
        ),
        in_specs=[smem, smem, pl.BlockSpec(memory_space=pltpu.VMEM), hbm, hbm, hbm],
        out_specs=(hbm, hbm),
        scratch_shapes=[
            pltpu.VMEM((slot, qwidth), bf16),
            pltpu.VMEM((slot, qwidth), bf16),
            pltpu.VMEM((slot, qwidth), bf16),
            pltpu.VMEM((rows, kv2), bf16),
            *blocks, *blocks, *blocks,
            *[pltpu.VMEM((k, rows, 2 * w), bf16) for k, w in zip(SUM_SLOTS, width)],
            *(grads * 6),
            dma((2,)), dma((STEPS,)), dma((STEPS,)), dma((STEPS, 2)),
            dma((nt, STEPS)), dma((KV_SLOTS, STEPS)), dma((max(SUM_SLOTS), STEPS)), dma((nt, STEPS)),
            *([dma((STEPS,))] * 6),
        ],
        compiler_params=pltpu.CompilerParams(
            collective_id=0, has_side_effects=True, vmem_limit_bytes=60 * 1024 * 1024
        ),
        name="attention_grads",
    )(
        lengths,
        route,
        advantage.reshape(1, slot),
        queries.reshape(slot, qwidth),
        keys_values.reshape(rows, kv2),
        cotangent.reshape(slot, qwidth),
    )
    return dq.reshape(slot, 1, qwidth), dkv.reshape(rows, 1, kv2)


def solution(mesh):
    placed = (
        P(None, "dp", "tensor"),
        P("tensor", "dp", None),
        P(),
        P(),
        P(None, "dp", "tensor"),
        P(None, "dp"),
    )
    return jax.shard_map(
        on_device,
        mesh=mesh,
        in_specs=placed,
        out_specs=(P(None, "dp", "tensor"), P("tensor", "dp", None)),
        check_vma=False,
    )
```

time: 183 us -> 51.3 us (0.28)
  the two profiles are of different devices: /device:TPU:4 before, /device:TPU:8 now
where the time goes in v2:
time: 51.3 us; the launch traced here: 51.1 us
  Pallas kernels  47.3 us (92%)
  local copies, waits for them, and re-layouts  2.46 us (5%)
  between operations  1.29 us (3%)
    pallas_call x1, Pallas kernels, on_device(): pl.pallas_call(functools.partial(kernel, nt, nh), out_shape=(jax.ShapeDty...  47.3 us
    unnamed x4, local copies, waits for them, and re-layouts  2.46 us

profile of v2, /device:TPU:8, one launch (start us, length us, event | category | flops | bytes accessed | tf_op | source)
XLA Modules:
  0.0 51.1 jit_solution(3781926294296917793)
XLA Ops:
  1.3 47.3 %attention_grads.1 = (bf16[192,1024]{1,0:T(8,128)(2,1)}, bf16[32,2048]{1,0:T(8,128)(2,1)}) custom-call(s32[128]{0:T(128)} %len_ref.1, s32[1]{0:T(128)S(6)} %copy.10.route_ref, s32[1,192]{1,0:T(1,128)} %bitcast.11, bf16[192,1024]{1,0:T(8,128)(2,1)} %bitcast.6, bf16[32,2048]{1,0:T(8,128)(2,1)} %bitcast.9, bf16[192,1024]{1,0:T(8,128)(2,1)} %bitcast.7), custom_call_target="tpu_custom_call" | custom-call | tf_op jit(solution)/shard_map/attention_grads/pallas_call | solution.py:371
  48.6 0.0 copy-start
  48.6 1.8 %copy.11 = bf16[192,1,1024]{2,0,1:T(8,128)(2,1)} copy(bf16[192,1,1024]{2,0,1:T(8,128)(2,1)} %bitcast.8) | data formatting | bytes 786432
  50.4 0.0 copy-done
  50.4 0.7 %copy.12 = bf16[32,1,2048]{2,0,1:T(8,128)(2,1)} copy(bf16[32,1,2048]{2,0,1:T(8,128)(2,1)S(1)} %bitcast.10) | data formatting | bytes 262144
Async XLA Ops:
  48.6 1.8 %copy-start = (bf16[32,2048]{1,0:T(8,128)(2,1)S(1)}, bf16[32,2048]{1,0:T(8,128)(2,1)}, u32[]{:S(2)}) copy-start(bf16[32,2048]{1,0:T(8,128)(2,1)} %get-tuple-element.5) | copy-start | bytes 393220

commit v3 on v2

--- a/solution.py
+++ b/solution.py
@@ -19,25 +19,25 @@
 
 
 LINE = 6
-HEADS = (1, 2, 2, 2, 1)
-AHEAD = 1
-ISSUED = 2
-RELAY_LAG = 1
-FINISH_LAG = 2
+HEADS = (2, 2, 2, 2)
+AHEAD = 2
+ISSUED = 4
+RELAY_LAG = 2
+FINISH_LAG = 4
 
 TWO_STOPS = ((0, 1, 0, 3, 3), (1, 2, 1, 4), (2, 2, 4), (3, 4), (4,))
-KV_TREES = (TWO_STOPS,) * len(HEADS)
-SUM_TREES = (TWO_STOPS,) * len(HEADS)
-
-
-def plan(tree):
+KV_TREES = ((TWO_STOPS, TWO_STOPS),) * len(HEADS)
+SUM_TREES = ((TWO_STOPS, TWO_STOPS),) * len(HEADS)
+
+
+def plan(trees, key):
+    above, below = trees
     copies = []
-    for s, parents in enumerate(tree):
-        for i, a in enumerate(parents):
-            b = s + 1 + i
-            copies.append((s, a, b))
-            copies.append((LINE - 1 - s, LINE - 1 - a, LINE - 1 - b))
-    copies.sort(key=lambda c: (abs(c[0] - c[1]), -abs(c[0] - c[2]), c))
+    for s, parents in enumerate(above):
+        copies += [(s, a, s + 1 + i) for i, a in enumerate(parents)]
+    for s, parents in enumerate(below):
+        copies += [(LINE - 1 - s, LINE - 1 - a, LINE - 2 - s - i) for i, a in enumerate(parents)]
+    copies.sort(key=key)
     used = [0] * LINE
     edges = []
     for s, a, b in copies:
@@ -46,6 +46,11 @@
     return edges
 
 
+def far_last(copy):
+    s, a, b = copy
+    return (abs(s - a), -abs(s - b), copy)
+
+
 def outgoing(edges, s, a):
     return [e for e in edges if e[0] == s and e[1] == a]
 
@@ -56,8 +61,8 @@
 
 STEPS = len(HEADS)
 FIRST = [sum(HEADS[:n]) for n in range(STEPS)]
-KV_EDGES = [plan(tree) for tree in KV_TREES]
-SUM_EDGES = [plan(tree) for tree in SUM_TREES]
+KV_EDGES = [plan(trees, far_last) for trees in KV_TREES]
+SUM_EDGES = [plan(trees, lambda copy: copy) for trees in SUM_TREES]
 KV_SLOTS = 1 + max(e[3] for edges in KV_EDGES for e in edges)
 SUM_SLOTS = [1 + max(e[3] for e in edges) for edges in SUM_EDGES]
 PARTNERS = {frozenset((e[1], e[2])) for edges in KV_EDGES + SUM_EDGES for e in edges}
@@ -70,7 +75,7 @@
     return found
 
 
-def kernel(nt, nh, len_ref, route_ref, adv_ref, q_hbm, kv_hbm, cot_hbm, dq_hbm, dkv_hbm, *scratch):
+def kernel(nt, nh, len_hbm, route_hbm, adv_hbm, q_hbm, kv_hbm, cot_hbm, dq_hbm, dkv_hbm, *scratch):
     scratch = list(scratch)
 
     def take(count):
@@ -78,7 +83,7 @@
         del scratch[:count]
         return taken
 
-    q, cot, dqb, dkvb = take(4)
+    len_ref, route_ref, adv_ref, q, cot, dqb, dkvb = take(7)
     kvb, part, sums, arrived = take(STEPS), take(STEPS), take(STEPS), take(STEPS)
     g0, gsib, sel1, ga, sela, gb = [take(STEPS) for _ in range(6)]
     in_sem, own_sem, dq_sem, dkv_sem = take(4)
@@ -161,16 +166,13 @@
             pltpu.make_async_copy(kv_hbm.at[:, there], kvb[n].at[band(t), here], own_sem.at[n]).start()
 
     def direct(n):
+        own(n).wait()
         for edge in KV_EDGES[n]:
-            s, a, b, k = edge
-            if s == a:
-
-                @pl.when(t == a)
+            if edge[0] == edge[1]:
+
+                @pl.when(t == edge[1])
                 def _():
-                    for there, here in halves(n):
-                        remote(
-                            kv_hbm.at[:, there], kvb[n].at[band(s), here], kv_s.at[k, n], kv_r.at[s, n], dp, b
-                        ).start()
+                    kv_copy(edge, n).start()
 
     def relay(n):
         for s, a in stops(KV_EDGES[n]):
@@ -182,7 +184,6 @@
                     kv_copy(edge, n).start()
 
     def arrive(n):
-        own(n).wait()
         for s in range(nt):
             leaves = [m for m in range(nt) if m != s and not outgoing(KV_EDGES[n], s, m)]
 
@@ -192,14 +193,22 @@
 
     load_cot = pltpu.make_async_copy(cot_hbm, cot, in_sem.at[0])
     load_q = pltpu.make_async_copy(q_hbm, q, in_sem.at[1])
+    for n in range(STEPS):
+        load_own(n)
     load_cot.start()
+    small = [
+        pltpu.make_async_copy(src, dst, in_sem.at[2 + i])
+        for i, (src, dst) in enumerate(((len_hbm, len_ref), (route_hbm, route_ref), (adv_hbm, adv_ref)))
+    ]
+    for copy in small:
+        copy.start()
     pl.semaphore_wait(barrier, greetings)
     for n in range(min(ISSUED, STEPS)):
         direct(n)
-    for n in range(STEPS):
-        load_own(n)
     load_q.start()
 
+    for copy in small:
+        copy.wait()
     code = route_ref[0]
     moved = jnp.bitwise_xor(dp, code)
     slot_len = len_ref[moved]
@@ -282,7 +291,7 @@
         return total.astype(jnp.bfloat16)
 
     def relay_sums(n):
-        for s, a in reversed(stops(SUM_EDGES[n])):
+        for s, a in sorted(stops(SUM_EDGES[n])):
             into = [e for e in SUM_EDGES[n] if e[0] == s and e[2] == a][0]
 
             @pl.when(t == a)
@@ -356,6 +365,27 @@
         store_dkv(n, 1).wait()
 
 
+def deliver(dq_in, dkv_in, dq_out, dkv_out, dq, dkv, in_sem, out_sem):
+    pieces = [(dq_in, dq, dq_out, 96, i) for i in range(dq.shape[0] // 96)]
+    pieces += [(dkv_in, dkv, dkv_out, 32, i) for i in range(dkv.shape[0] // 32)]
+    stages = []
+    for k, (src, mid, dst, rows, i) in enumerate(pieces):
+        piece = pl.ds(i * rows, rows)
+        stages.append(
+            (
+                pltpu.make_async_copy(src.at[piece], mid.at[piece], in_sem.at[k]),
+                pltpu.make_async_copy(mid.at[piece], dst.at[piece], out_sem.at[k]),
+            )
+        )
+    for load, _ in stages:
+        load.start()
+    for load, store in stages:
+        load.wait()
+        store.start()
+    for _, store in stages:
+        store.wait()
+
+
 def on_device(queries, keys_values, lengths, route, cotangent, advantage):
     slot, _, qwidth = queries.shape
     rows, _, kv2 = keys_values.shape
@@ -363,7 +393,6 @@
     nh = kv2 // 2 // HEAD_DIM
     bf16 = jnp.bfloat16
     dma = pltpu.SemaphoreType.DMA
-    smem = pl.BlockSpec(memory_space=pltpu.SMEM)
     hbm = pl.BlockSpec(memory_space=pl.ANY)
     width = [h * HEAD_DIM for h in HEADS]
     blocks = [pltpu.VMEM((slot, 2 * w), bf16) for w in width]
@@ -374,9 +403,12 @@
             jax.ShapeDtypeStruct((slot, qwidth), bf16),
             jax.ShapeDtypeStruct((rows, kv2), bf16),
         ),
-        in_specs=[smem, smem, pl.BlockSpec(memory_space=pltpu.VMEM), hbm, hbm, hbm],
+        in_specs=[hbm] * 6,
         out_specs=(hbm, hbm),
         scratch_shapes=[
+            pltpu.SMEM(lengths.shape, jnp.int32),
+            pltpu.SMEM(route.shape, jnp.int32),
+            pltpu.VMEM((1, slot), jnp.int32),
             pltpu.VMEM((slot, qwidth), bf16),
             pltpu.VMEM((slot, qwidth), bf16),
             pltpu.VMEM((slot, qwidth), bf16),
@@ -384,7 +416,7 @@
             *blocks, *blocks, *blocks,
             *[pltpu.VMEM((k, rows, 2 * w), bf16) for k, w in zip(SUM_SLOTS, width)],
             *(grads * 6),
-            dma((2,)), dma((STEPS,)), dma((STEPS,)), dma((STEPS, 2)),
+            dma((5,)), dma((STEPS,)), dma((STEPS,)), dma((STEPS, 2)),
             dma((nt, STEPS)), dma((KV_SLOTS, STEPS)), dma((max(SUM_SLOTS), STEPS)), dma((nt, STEPS)),
             *([dma((STEPS,))] * 6),
         ],
@@ -400,6 +432,20 @@
         keys_values.reshape(rows, kv2),
         cotangent.reshape(slot, qwidth),
     )
+    dq, dkv = pl.pallas_call(
+        deliver,
+        out_shape=(jax.ShapeDtypeStruct(dq.shape, bf16), jax.ShapeDtypeStruct(dkv.shape, bf16)),
+        in_specs=[hbm, hbm],
+        out_specs=(hbm, hbm),
+        scratch_shapes=[
+            pltpu.VMEM(dq.shape, bf16),
+            pltpu.VMEM(dkv.shape, bf16),
+            dma((slot // 96 + rows // 32,)),
+            dma((slot // 96 + rows // 32,)),
+        ],
+        compiler_params=pltpu.CompilerParams(vmem_limit_bytes=60 * 1024 * 1024),
+        name="deliver",
+    )(dq, dkv)
     return dq.reshape(slot, 1, qwidth), dkv.reshape(rows, 1, kv2)
 
 

time: 51.3 us -> 48.2 us (0.940)
  the two profiles are of different devices: /device:TPU:8 before, /device:TPU:102 now
where the time goes in v3:
time: 48.2 us; the launch traced here: 48 us
  Pallas kernels  46.7 us (97%)
  between operations  1.29 us (3%)
    pallas_call x1, Pallas kernels, on_device(): pl.pallas_call(functools.partial(kernel, nt, nh), out_shape=(jax.ShapeDty...  44.9 us
    pallas_call x1, Pallas kernels, on_device(): pl.pallas_call(deliver, out_shape=(jax.ShapeDtypeStruct(dq.shape, bf16),...  1.8 us

profile of v3, /device:TPU:102, one launch (start us, length us, event | category | flops | bytes accessed | tf_op | source)
XLA Modules:
  0.0 48.0 jit_solution(1911292280380914695)
XLA Ops:
  1.3 44.9 %attention_grads.1 = (bf16[192,1024]{1,0:T(8,128)(2,1)}, bf16[32,2048]{1,0:T(8,128)(2,1)}) custom-call(s32[128]{0:T(128)} %len_hbm.1, s32[1]{0:T(128)S(6)} %copy.8.route_hbm, s32[1,192]{1,0:T(1,128)} %bitcast.9, bf16[192,1024]{1,0:T(8,128)(2,1)} %bitcast.6, bf16[32,2048]{1,0:T(8,128)(2,1)} %bitcast.8, bf16[192,1024]{1,0:T(8,128)(2,1)} %bitcast.7), custom_call_target="tpu_custom_call" | custom-call | tf_op jit(solution)/shard_map/attention_grads/pallas_call | solution.py:400
  46.2 1.8 %deliver.1 = (bf16[192,1024]{1,0:T(8,128)(2,1)}, bf16[32,2048]{1,0:T(8,128)(2,1)}) custom-call(bf16[192,1024]{1,0:T(8,128)(2,1)} %get-tuple-element.6.dq_in, bf16[32,2048]{1,0:T(8,128)(2,1)} %get-tuple-element.7.dkv_in), custom_call_target="tpu_custom_call" | custom-call | tf_op jit(solution)/shard_map/deliver/pallas_call | solution.py:435

commit v4 on v3

--- a/solution.py
+++ b/solution.py
@@ -20,7 +20,7 @@
 
 LINE = 6
 HEADS = (2, 2, 2, 2)
-AHEAD = 2
+AHEAD = 1
 ISSUED = 4
 RELAY_LAG = 2
 FINISH_LAG = 4
@@ -334,9 +334,10 @@
             def _():
                 kv_copy(edge, n).wait_send()
 
+    hop_b(0)
     for n in range(AHEAD):
         relay(n)
-    hop_b(0)
+    hop_b(1)
     load_q.wait()
 
     for n in range(STEPS + FINISH_LAG):
@@ -344,8 +345,8 @@
             direct(n + ISSUED)
         if n + AHEAD < STEPS:
             relay(n + AHEAD)
-        if n + 1 < STEPS:
-            hop_b(n + 1)
+        if n + 2 < STEPS:
+            hop_b(n + 2)
         if n < STEPS:
             arrive(n)
             compute(n)

time: 48.2 us -> 47 us (0.975)
  the two profiles are of different devices: /device:TPU:102 before, /device:TPU:12 now
where the time goes in v4:
time: 47 us; the launch traced here: 46.8 us
  Pallas kernels  45.5 us (97%)
  between operations  1.29 us (3%)
    pallas_call x1, Pallas kernels, on_device(): pl.pallas_call(functools.partial(kernel, nt, nh), out_shape=(jax.ShapeDty...  43.7 us
    pallas_call x1, Pallas kernels, on_device(): pl.pallas_call(deliver, out_shape=(jax.ShapeDtypeStruct(dq.shape, bf16),...  1.8 us

profile of v4, /device:TPU:12, one launch (start us, length us, event | category | flops | bytes accessed | tf_op | source)
XLA Modules:
  0.0 46.8 jit_solution(2220114310373183625)
XLA Ops:
  1.3 43.7 %attention_grads.1 = (bf16[192,1024]{1,0:T(8,128)(2,1)}, bf16[32,2048]{1,0:T(8,128)(2,1)}) custom-call(s32[128]{0:T(128)} %len_hbm.1, s32[1]{0:T(128)S(6)} %copy.8.route_hbm, s32[1,192]{1,0:T(1,128)} %bitcast.9, bf16[192,1024]{1,0:T(8,128)(2,1)} %bitcast.6, bf16[32,2048]{1,0:T(8,128)(2,1)} %bitcast.8, bf16[192,1024]{1,0:T(8,128)(2,1)} %bitcast.7), custom_call_target="tpu_custom_call" | custom-call | tf_op jit(solution)/shard_map/attention_grads/pallas_call | solution.py:401
  45.0 1.8 %deliver.1 = (bf16[192,1024]{1,0:T(8,128)(2,1)}, bf16[32,2048]{1,0:T(8,128)(2,1)}) custom-call(bf16[192,1024]{1,0:T(8,128)(2,1)} %get-tuple-element.6.dq_in, bf16[32,2048]{1,0:T(8,128)(2,1)} %get-tuple-element.7.dkv_in), custom_call_target="tpu_custom_call" | custom-call | tf_op jit(solution)/shard_map/deliver/pallas_call | solution.py:436
